TPU v7x, 32 devices: a whole 2x2x4 slice. The times are simulated.
32 devices in a mesh: seq: 4 (over x, core), batch: 8 (over z, y).
Axes of the slice: x: 2, y: 2, z: 4, core: 2. Of those that a mesh axis runs over, the one named last changes fastest.
Arguments:
- block_input: bfloat16 [16, 1024, 768], P('batch', 'seq'), may hold values from -6 to 6
- lengths: int32 [16], P('batch'), may hold values from 1 to 1024, as said below
- pass_ids: int32 [16, 1024], P('batch', 'seq'), may hold values from 0 to 4
- pass_embed: float32 [5, 768], replicated, may hold values from -3 to 3
- ln1_gain: float32 [768], replicated, may hold values from 0.5 to 1.5
- ln1_bias: float32 [768], replicated, may hold values from -1.2 to 1.2
- w_qkv: bfloat16 [768, 2304], replicated, may hold values from -0.21875 to 0.21875
- w_out: bfloat16 [768, 768], replicated, may hold values from -1.75 to 1.75
- ln2_gain: float32 [768], replicated, may hold values from 0.5 to 1.5
- ln2_bias: float32 [768], replicated, may hold values from -1.2 to 1.2
- w_up: bfloat16 [768, 3072], replicated, may hold values from -0.21875 to 0.21875
- b_up: float32 [3072], replicated, may hold values from -1.8 to 1.8
- w_down: bfloat16 [3072, 768], replicated, may hold values from -0.109375 to 0.109375
- b_down: float32 [768], replicated, may hold values from -1.8 to 1.8
- cotangent: bfloat16 [16, 1024, 768], P('batch', 'seq'), may hold values from -6 to 6
Outputs:
- output: bfloat16 [16, 1024, 768], P('batch', 'seq')
- grad_input: bfloat16 [16, 1024, 768], P('batch', 'seq')
- grad_pass_embed: float32 [5, 768], replicated
- grad_ln1_gain: float32 [768], replicated
- grad_ln1_bias: float32 [768], replicated
- grad_w_qkv: float32 [768, 2304], P('seq', 'batch')
- grad_w_out: float32 [768, 768], P('seq', 'batch')
- grad_ln2_gain: float32 [768], replicated
- grad_ln2_bias: float32 [768], replicated
- grad_w_up: float32 [768, 3072], P('seq', 'batch')
- grad_b_up: float32 [3072], replicated
- grad_w_down: float32 [3072, 768], P('seq', 'batch')
- grad_b_down: float32 [768], replicated
Inputs may be any that keep to these rules, and one draw needn't show every extreme that they name: `lengths`: in each aligned block of 2 rows one row, drawn from the seed, has all 1024 positions.
All inputs are finite; a program needn't handle non-finite values.
Results may differ from a plain program's by a relative error of at most 0.019.
Values may be sent and summed in bfloat16 or wider, within the bound.
A program may use at most 192 MiB of HBM per device.

v0:
```python
import jax
import jax.numpy as jnp
from jax import lax
from jax.sharding import PartitionSpec as P

H = 12


negative = -1e30
key_block = 1024
query_block = 512
highest = lax.Precision.HIGHEST


def layer_norm(hidden, gain, offset):
    centre = jnp.mean(hidden, -1, keepdims=True)
    shifted = hidden - centre
    spread = jnp.mean(shifted * shifted, -1, keepdims=True)
    return shifted * lax.rsqrt(spread + 1e-05) * gain + offset


def gelu_tanh(values):
    return jax.nn.gelu(values, approximate=True)


def visible(query_place, query_pass, key_place, key_pass, length):
    earlier = key_place[None, :] < query_place[:, None]
    allowed = earlier & (key_pass[None, :] <= query_pass[:, None]) & (key_place[None, :] < length)
    return allowed | (key_place[None, :] == query_place[:, None])


def masked_scores(query_part, key_part, factor, seen):
    raw = (
        jnp.einsum("qhd,khd->hqk", query_part, key_part, preferred_element_type=jnp.float32)
        * factor
    )
    return jnp.where(seen[None], raw, negative)


def split_blocks(arrays, block_len):
    return tuple(
        (
            array.reshape((array.shape[0] // block_len, block_len) + array.shape[1:])
            for array in arrays
        )
    )


def chance_of(query_part, key_part, log_part, seen, factor):
    scores = masked_scores(query_part, key_part, factor, seen)
    return jnp.where(seen[None], jnp.exp(scores - log_part[..., None]), 0.0)


def grad_pieces(query_part, dout_part, log_part, delta_part, key_part, value_part, seen, factor):
    chance = chance_of(query_part, key_part, log_part, seen, factor)
    dprob = jnp.einsum("qhd,khd->hqk", dout_part, value_part, preferred_element_type=jnp.float32)
    dscore = (chance * (dprob - delta_part[..., None])).astype(jnp.bfloat16)
    return (dscore, chance.astype(jnp.bfloat16))


def attend_row(queries, query_place, query_pass, key_rows, value_rows, key_pass, length):
    factor = queries.shape[-1] ** (-0.5)
    places = jnp.arange(key_rows.shape[0], dtype=jnp.int32)
    key_parts = split_blocks(
        (key_rows, value_rows, key_pass, places), min(key_block, key_rows.shape[0])
    )
    query_len = min(query_block, queries.shape[0])
    query_parts = split_blocks((queries, query_place, query_pass), query_len)

    def attend_one_block(query_args):
        query_part, place_part, pass_part = query_args

        def running(carry, key_args):
            peak, summed, total_out = carry
            key_part, value_part, kpass_part, kplace_part = key_args
            seen = visible(place_part, pass_part, kplace_part, kpass_part, length)
            scores = masked_scores(query_part, key_part, factor, seen)
            new_peak = jnp.maximum(peak, jnp.max(scores, -1))
            terms = jnp.where(seen[None], jnp.exp(scores - new_peak[..., None]), 0.0)
            rescale = jnp.exp(peak - new_peak)
            summed = summed * rescale + jnp.sum(terms, -1)
            added = jnp.einsum(
                "hqk,khd->qhd",
                terms.astype(jnp.bfloat16),
                value_part,
                preferred_element_type=jnp.float32,
            )
            total_out = total_out * rescale.T[..., None] + added
            return ((new_peak, summed, total_out), None)

        heads_n = query_part.shape[1]
        start = (
            jnp.full((heads_n, query_len), negative, jnp.float32),
            jnp.zeros((heads_n, query_len), jnp.float32),
            jnp.zeros(query_part.shape, jnp.float32),
        )
        (peak, summed, total_out), _ = lax.scan(running, start, key_parts)
        log_total = peak + jnp.log(summed)
        result = total_out / summed.T[..., None]
        return (result, log_total)

    results, log_totals = lax.map(attend_one_block, query_parts)
    heads_n = queries.shape[1]
    return (
        results.reshape(queries.shape),
        jnp.moveaxis(log_totals, 1, 0).reshape(heads_n, queries.shape[0]),
    )


def backward_row(
    queries,
    douts,
    outs_kept,
    log_totals,
    query_place,
    query_pass,
    key_rows,
    value_rows,
    key_pass,
    length,
):
    factor = queries.shape[-1] ** (-0.5)
    places = jnp.arange(key_rows.shape[0], dtype=jnp.int32)
    key_parts = split_blocks(
        (key_rows, value_rows, key_pass, places), min(key_block, key_rows.shape[0])
    )
    query_len = min(query_block, queries.shape[0])
    heads_n = queries.shape[1]
    block_count = queries.shape[0] // query_len
    log_parts = jnp.moveaxis(log_totals.reshape(heads_n, block_count, query_len), 1, 0)
    query_parts = split_blocks((queries, douts, outs_kept, query_place, query_pass), query_len)

    def backward_one_block(carry, query_args):
        query_part, dout_part, kept_part, place_part, pass_part, log_part = query_args
        delta_part = jnp.einsum("qhd,qhd->hq", dout_part.astype(jnp.float32), kept_part)

        def add_grads(dquery, key_args):
            key_part, value_part, kpass_part, kplace_part = key_args
            seen = visible(place_part, pass_part, kplace_part, kpass_part, length)
            dscore, low_chance = grad_pieces(
                query_part, dout_part, log_part, delta_part, key_part, value_part, seen, factor
            )
            dquery = dquery + factor * jnp.einsum(
                "hqk,khd->qhd", dscore, key_part, preferred_element_type=jnp.float32
            )
            dkey = factor * jnp.einsum(
                "hqk,qhd->khd", dscore, query_part, preferred_element_type=jnp.float32
            )
            dvalue = jnp.einsum(
                "hqk,qhd->khd", low_chance, dout_part, preferred_element_type=jnp.float32
            )
            return (dquery, (dkey, dvalue))

        dquery, key_terms = lax.scan(add_grads, jnp.zeros(query_part.shape, jnp.float32), key_parts)
        carry = (
            carry[0] + key_terms[0].reshape(key_rows.shape),
            carry[1] + key_terms[1].reshape(value_rows.shape),
        )
        return (carry, (dquery, delta_part))

    start = (jnp.zeros(key_rows.shape, jnp.float32), jnp.zeros(value_rows.shape, jnp.float32))
    key_sums, (dqueries, deltas) = lax.scan(backward_one_block, start, query_parts + (log_parts,))
    return (
        dqueries.reshape(queries.shape),
        jnp.moveaxis(deltas, 1, 0).reshape(heads_n, queries.shape[0]),
        key_sums,
    )


def local(
    block_input,
    lengths,
    pass_ids,
    pass_embed,
    ln1_gain,
    ln1_bias,
    w_qkv,
    w_out,
    ln2_gain,
    ln2_bias,
    w_up,
    b_up,
    w_down,
    b_down,
    cotangent,
):
    row_count, seg_len, width = block_input.shape
    heads_n = H
    head_size = width // heads_n
    onehot = (
        pass_ids[..., None] == jnp.arange(pass_embed.shape[0], dtype=jnp.int32)[None, None, :]
    ).astype(jnp.float32)
    hidden_in = block_input.astype(jnp.float32) + jnp.einsum(
        "rsp,pd->rsd", onehot, pass_embed, precision=highest
    )
    normed, norm_back = jax.vjp(layer_norm, hidden_in, ln1_gain, ln1_bias)
    normed_low = normed.astype(jnp.bfloat16)
    qkv = jnp.einsum("rsd,de->rse", normed_low, w_qkv, preferred_element_type=jnp.float32)
    queries = qkv[..., :width].astype(jnp.bfloat16)
    key_flat = qkv[..., width : 2 * width].astype(jnp.bfloat16)
    value_flat = qkv[..., 2 * width :].astype(jnp.bfloat16)
    pass_low = pass_ids.astype(jnp.bfloat16)
    key_all, value_all, pass_all = (
        lax.all_gather(key_flat, "seq", axis=1, tiled=True),
        lax.all_gather(value_flat, "seq", axis=1, tiled=True),
        lax.all_gather(pass_low, "seq", axis=1, tiled=True),
    )
    total_len = key_all.shape[1]
    key_all = key_all.reshape(row_count, total_len, heads_n, head_size)
    value_all = value_all.reshape(row_count, total_len, heads_n, head_size)
    pass_all = pass_all.astype(jnp.float32)
    offset = lax.axis_index("seq") * seg_len
    query_place = offset + jnp.arange(seg_len, dtype=jnp.int32)
    query_pass = pass_ids.astype(jnp.float32)
    query_heads = queries.reshape(row_count, seg_len, heads_n, head_size)
    attended_rows = []
    log_rows = []
    for row in range(row_count):
        attended, log_total = attend_row(
            query_heads[row],
            query_place,
            query_pass[row],
            key_all[row],
            value_all[row],
            pass_all[row],
            lengths[row],
        )
        attended_rows.append(attended)
        log_rows.append(log_total)
    attended_low = jnp.stack(attended_rows).astype(jnp.bfloat16).reshape(row_count, seg_len, width)
    branch = jnp.einsum("rsd,de->rse", attended_low, w_out, preferred_element_type=jnp.float32)
    middle = hidden_in + branch
    normed2, norm2_back = jax.vjp(layer_norm, middle, ln2_gain, ln2_bias)
    normed2_low = normed2.astype(jnp.bfloat16)
    pre_act = (
        jnp.einsum("rsd,df->rsf", normed2_low, w_up, preferred_element_type=jnp.float32) + b_up
    )
    active, active_back = jax.vjp(gelu_tanh, pre_act)
    active_low = active.astype(jnp.bfloat16)
    result = (
        middle
        + jnp.einsum("rsf,fd->rsd", active_low, w_down, preferred_element_type=jnp.float32)
        + b_down
    )
    output = result.astype(jnp.bfloat16)
    cot_f = cotangent.astype(jnp.float32)
    grad_active = jnp.einsum("rsd,fd->rsf", cotangent, w_down, preferred_element_type=jnp.float32)
    grad_w_down = jnp.einsum(
        "rsf,rsd->fd", active_low, cotangent, preferred_element_type=jnp.float32
    )
    grad_b_down = jnp.sum(cot_f, (0, 1))
    grad_pre = active_back(grad_active)[0].astype(jnp.bfloat16)
    grad_b_up = jnp.sum(grad_pre.astype(jnp.float32), (0, 1))
    grad_w_up = jnp.einsum("rsd,rsf->df", normed2_low, grad_pre, preferred_element_type=jnp.float32)
    grad_normed2 = jnp.einsum("rsf,df->rsd", grad_pre, w_up, preferred_element_type=jnp.float32)
    grad_mid_norm, grad_ln2_gain, grad_ln2_bias = norm2_back(grad_normed2)
    grad_middle = cot_f + grad_mid_norm
    grad_branch = grad_middle.astype(jnp.bfloat16)
    grad_w_out = jnp.einsum(
        "rsd,rse->de", attended_low, grad_branch, preferred_element_type=jnp.float32
    )
    grad_attended = jnp.einsum(
        "rse,de->rsd", grad_branch, w_out, preferred_element_type=jnp.float32
    ).astype(jnp.bfloat16)
    dout_heads = grad_attended.reshape(row_count, seg_len, heads_n, head_size)
    dquery_rows = []
    dkey_rows = []
    dvalue_rows = []
    for row in range(row_count):
        dquery, _, key_sums = backward_row(
            query_heads[row],
            dout_heads[row],
            attended_rows[row],
            log_rows[row],
            query_place,
            query_pass[row],
            key_all[row],
            value_all[row],
            pass_all[row],
            lengths[row],
        )
        dquery_rows.append(dquery)
        dkey_rows.append(key_sums[0].reshape(total_len, width))
        dvalue_rows.append(key_sums[1].reshape(total_len, width))
    dkey_sum, dvalue_sum = (
        lax.psum_scatter(
            jnp.stack(dkey_rows).astype(jnp.bfloat16), "seq", scatter_dimension=1, tiled=True
        ).astype(jnp.float32),
        lax.psum_scatter(
            jnp.stack(dvalue_rows).astype(jnp.bfloat16), "seq", scatter_dimension=1, tiled=True
        ).astype(jnp.float32),
    )
    dquery_all = jnp.stack(dquery_rows).reshape(row_count, seg_len, width)
    grad_qkv = jnp.concatenate(
        [
            dquery_all.astype(jnp.bfloat16),
            dkey_sum.astype(jnp.bfloat16),
            dvalue_sum.astype(jnp.bfloat16),
        ],
        -1,
    )
    grad_w_qkv = jnp.einsum("rsd,rse->de", normed_low, grad_qkv, preferred_element_type=jnp.float32)
    grad_normed = jnp.einsum("rse,de->rsd", grad_qkv, w_qkv, preferred_element_type=jnp.float32)
    grad_in_norm, grad_ln1_gain, grad_ln1_bias = norm_back(grad_normed)
    grad_hidden = grad_middle + grad_in_norm
    grad_input = grad_hidden.astype(jnp.bfloat16)
    grad_pass = jnp.einsum("rsp,rsd->pd", onehot, grad_hidden, precision=highest)
    matrices = (
        lax.psum_scatter(
            grad_w_qkv.astype(jnp.bfloat16), "seq", scatter_dimension=0, tiled=True
        ).astype(jnp.float32),
        lax.psum_scatter(
            grad_w_out.astype(jnp.bfloat16), "seq", scatter_dimension=0, tiled=True
        ).astype(jnp.float32),
        lax.psum_scatter(
            grad_w_up.astype(jnp.bfloat16), "seq", scatter_dimension=0, tiled=True
        ).astype(jnp.float32),
        lax.psum_scatter(
            grad_w_down.astype(jnp.bfloat16), "seq", scatter_dimension=0, tiled=True
        ).astype(jnp.float32),
    )
    matrices = (
        lax.psum_scatter(
            matrices[0].astype(jnp.bfloat16), "batch", scatter_dimension=1, tiled=True
        ).astype(jnp.float32),
        lax.psum_scatter(
            matrices[1].astype(jnp.bfloat16), "batch", scatter_dimension=1, tiled=True
        ).astype(jnp.float32),
        lax.psum_scatter(
            matrices[2].astype(jnp.bfloat16), "batch", scatter_dimension=1, tiled=True
        ).astype(jnp.float32),
        lax.psum_scatter(
            matrices[3].astype(jnp.bfloat16), "batch", scatter_dimension=1, tiled=True
        ).astype(jnp.float32),
    )
    vectors = lax.psum(
        (
            grad_pass,
            grad_ln1_gain,
            grad_ln1_bias,
            grad_ln2_gain,
            grad_ln2_bias,
            grad_b_up,
            grad_b_down,
        ),
        ("seq", "batch"),
    )
    return (
        output,
        grad_input,
        vectors[0],
        vectors[1],
        vectors[2],
        matrices[0],
        matrices[1],
        vectors[3],
        vectors[4],
        matrices[2],
        vectors[5],
        matrices[3],
        vectors[6],
    )


def solution(mesh):
    return jax.shard_map(
        local,
        mesh=mesh,
        in_specs=(
            P("batch", "seq", None),
            P("batch"),
            P("batch", "seq"),
            P(),
            P(),
            P(),
            P(),
            P(),
            P(),
            P(),
            P(),
            P(),
            P(),
            P(),
            P("batch", "seq", None),
        ),
        out_specs=(
            P("batch", "seq", None),
            P("batch", "seq", None),
            P(),
            P(),
            P(),
            P("seq", "batch"),
            P("seq", "batch"),
            P(),
            P(),
            P("seq", "batch"),
            P(),
            P("seq", "batch"),
            P(),
        ),
        check_vma=False,
    )
```

profile of v0, /device:TPU:0, one launch (start us, length us, event | category | flops | bytes accessed | tf_op | source)
XLA Modules:
  0.0 665.9 jit_solution(18316141235244333976)
XLA Ops:
  21.9 6.4 all_gather.9
  34.3 11.9 %all-gather.3.cloned.1.call-done = bf16[2,1024,768]{2,1,0:T(8,128)(2,1)} async-done(((bf16[2,256,768]{2,1,0:T(8,128)(2,1)}), bf16[2,1024,768]{2,1,0:T(8,128)(2,1)}) %all-gather.3.cloned.1.call-update) | async-done | bytes 3145744 | tf_op jit(solution)/shard_map/all_gather | solution.py:204
  46.2 3.9 fusion.106
  55.3 4.2 fusion.7
  64.3 7.7 %fusion = (f32[12,256]{1,0:T(8,128)S(1)}, f32[12,256]{1,0:T(8,128)S(1)}) fusion(f32[12,256,1024]{2,1,0:T(8,128)S(1)} %get-tuple-element.474, f32[12,256]{1,0:T(8,128)S(1)} %broadcast_maximum_fusion.1, pred[256,1024]{1,0:T(8,128)(4,1)S(1)} %copy-done.16, f32[12,256]{1,0:T(8,128)S(1)} %broadcast_maximum_fusion, f32[12,256,1024]{2,1,0:T(8,128)S(1)} %get-tuple-element.470, ...), kind=kLoop, calls=%fused_computation.8 | loop fusion | flops 31451136 | bytes 25739264 | tf_op jit(solution)/shard_map/while/body/eval_jaxpr/while/body/eval_jaxpr/reduce_sum | solution.py:81
  76.9 3.8 fusion.107
  85.9 7.8 %fusion.116 = (bf16[256,12,64]{0,2,1:T(8,128)(2,1)}, f32[256,12,64]{0,2,1:T(8,128)}) fusion(f32[256,12]{0,1:T(8,128)} %bitcast_add_fusion, bf16[1024,12,64]{0,2,1:T(8,128)(2,1)} %bitcast.169, f32[12,256,1024]{2,1,0:T(8,128)} %copy-done.4, f32[12,256]{1,0:T(8,128)} %copy-done.22, pred[256,1024]{1,0:T(8,128)(4,1)} %get-tuple-element.464, ...), kind=kOutput, calls=%fused_computation.159 | convolution fusion | flops 418971648 | bytes 15634432 | tf_op jit(solution)/shard_map/while/body/eval_jaxpr/while/body/eval_jaxpr/hqk,khd->qhd/dot_general | solution.py:82
  95.7 8.0 %fusion.117 = (bf16[256,12,64]{0,2,1:T(8,128)(2,1)}, f32[256,12,64]{0,2,1:T(8,128)}) fusion(f32[256,12]{0,1:T(8,128)} %bitcast_add_fusion.1, bf16[1024,12,64]{0,2,1:T(8,128)(2,1)} %bitcast.167, f32[12,256,1024]{2,1,0:T(8,128)} %copy-done.3, f32[12,256]{1,0:T(8,128)S(1)} %broadcast_maximum_fusion.1, pred[256,1024]{1,0:T(8,128)(4,1)} %get-tuple-element.463, ...), kind=kOutput, calls=%fused_computation.160 | convolution fusion | flops 418971648 | bytes 15634432 | tf_op jit(solution)/shard_map/while/body/eval_jaxpr/while/body/eval_jaxpr/hqk,khd->qhd/dot_general | solution.py:82
  109.1 5.0 fusion.33
  114.1 7.2 %convert_reduce_fusion = (f32[3072]{0:T(1024)}, bf16[2,256,3072]{2,1,0:T(8,128)(2,1)S(1)}) fusion(f32[2,256,3072]{2,1,0:T(8,128)S(1)} %fusion.33, f32[3072]{0:T(1024)S(1)} %copy-done.35, bf16[2,256,768]{2,1,0:T(8,128)(2,1)S(1)} %copy-done.14, bf16[3072,768]{1,0:T(8,128)(2,1)S(1)} %bitcast.193), kind=kOutput, calls=%fused_computation.28 | convolution fusion | flops 2452091904 | bytes 14966784 | tf_op jit(solution)/shard_map/rsd,fd->rsf/dot_general | solution.py:247
  139.4 9.6 %fusion.43 = bf16[12,64,1024]{2,1,0:T(8,128)(2,1)} fusion(bf16[256,12,64]{0,2,1:T(8,128)(2,1)} %bitcast.177, f32[12,256,1024]{2,1,0:T(8,128)} %copy-done.4, f32[12,256]{1,0:T(8,128)} %get-tuple-element.455, pred[256,1024]{1,0:T(8,128)(4,1)} %get-tuple-element.464), kind=kOutput, calls=%fused_computation.61 | convolution fusion | flops 419168256 | bytes 14823424 | tf_op jit(solution)/shard_map/while/body/eval_jaxpr/while/body/eval_jaxpr/hqk,qhd->khd/dot_general | solution.py:149
  151.7 9.3 %fusion.40 = bf16[12,64,1024]{2,1,0:T(8,128)(2,1)} fusion(bf16[256,12,64]{0,2,1:T(8,128)(2,1)} %bitcast.174, f32[12,256,1024]{2,1,0:T(8,128)} %copy-done.3, f32[12,256]{1,0:T(8,128)} %get-tuple-element.453, pred[256,1024]{1,0:T(8,128)(4,1)} %get-tuple-element.463), kind=kOutput, calls=%fused_computation.60 | convolution fusion | flops 419168256 | bytes 14823424 | tf_op jit(solution)/shard_map/while/body/eval_jaxpr/while/body/eval_jaxpr/hqk,qhd->khd/dot_general | solution.py:149
  163.6 3.9 pad_maximum_fusion.1
  169.2 8.8 %multiply_convert_fusion = bf16[12,256,1024]{2,1,0:T(8,128)(2,1)S(1)} fusion(f32[12,256,1024]{2,1,0:T(8,128)} %copy-done.4, f32[12,256]{1,0:T(8,128)S(1)} %fusion.77, f32[12,256]{1,0:T(8,128)} %get-tuple-element.455, pred[256,1024]{1,0:T(8,128)(4,1)} %get-tuple-element.464, bf16[256,12,64]{0,2,1:T(8,128)(2,1)} %bitcast.179, bf16[1024,12,64]{0,2,1:T(8,128)(2,1)} %bitcast.170), kind=kOutput, calls=%fused_computation | convolution fusion | flops 424673280 | bytes 21127168 | tf_op jit(solution)/shard_map/while/body/eval_jaxpr/while/body/eval_jaxpr/qhd,khd->hqk/dot_general | solution.py:56
  185.0 9.1 %multiply_convert_fusion.1 = bf16[12,256,1024]{2,1,0:T(8,128)(2,1)S(1)} fusion(f32[12,256,1024]{2,1,0:T(8,128)} %copy-done.3, f32[12,256]{1,0:T(8,128)S(1)} %fusion.78, f32[12,256]{1,0:T(8,128)} %get-tuple-element.453, pred[256,1024]{1,0:T(8,128)(4,1)} %get-tuple-element.463, bf16[256,12,64]{0,2,1:T(8,128)(2,1)} %bitcast.176, bf16[1024,12,64]{0,2,1:T(8,128)(2,1)} %bitcast.168), kind=kOutput, calls=%fused_computation.2 | convolution fusion | flops 424673280 | bytes 21127168 | tf_op jit(solution)/shard_map/while/body/eval_jaxpr/while/body/eval_jaxpr/qhd,khd->hqk/dot_general | solution.py:56
  199.9 3.8 pad_maximum_fusion
  203.8 8.9 %bitcast_convert_fusion = bf16[3072,768]{1,0:T(8,128)(2,1)} fusion(bf16[2,256,768]{2,1,0:T(8,128)(2,1)} %param.29, f32[2,256,3072]{2,1,0:T(8,128)} %copy-done.38, f32[3072]{0:T(1024)} %param.26), kind=kOutput, calls=%fused_computation.14 | convolution fusion | flops 2434007040 | bytes 11808768 | tf_op jit(solution)/shard_map/rsf,rsd->fd/dot_general | solution.py:248
  213.0 7.6 %bitcast_convert_fusion.1 = bf16[768,3072]{1,0:T(8,128)(2,1)} fusion(bf16[2,256,3072]{2,1,0:T(8,128)(2,1)} %copy-done.39, f32[2,256,768]{2,1,0:T(8,128)} %copy-done.7, f32[768]{0:T(1024)} %param.24, f32[768]{0:T(1024)S(1)} %copy-done.33, f32[2,256]{1,0:T(2,128)S(1)} %fusion.86, f32[2,256]{1,0:T(2,128)S(1)} %broadcast_multiply_fusion), kind=kOutput, calls=%fused_computation.15 | convolution fusion | flops 2420244480 | bytes 9447424 | tf_op jit(solution)/shard_map/rsd,rsf->df/dot_general | solution.py:254
  220.6 6.1 fusion.61
  228.7 6.1 fusion.60
  238.6 7.6 %reduce-scatter.19.cloned.1.call-done = bf16[2,256,768]{2,1,0:T(8,128)(2,1)} async-done(((bf16[2,1024,768]{2,1,0:T(8,128)(2,1)}), bf16[2,256,768]{2,1,0:T(8,128)(2,1)}) %reduce-scatter.19.cloned.1.call-update) | async-done | bytes 786448 | tf_op jit(solution)/shard_map/reduce_scatter | solution.py:286
  246.1 6.1 bitcast_convert_fusion.2
  252.3 44.2 %reduce-scatter.29.cloned.1.call-done = bf16[768,768]{1,0:T(8,128)(2,1)} async-done(((bf16[3072,768]{1,0:T(8,128)(2,1)}), bf16[768,768]{1,0:T(8,128)(2,1)}) %reduce-scatter.29.cloned.1.call-update) | async-done | bytes 1179664 | tf_op jit(solution)/shard_map/reduce_scatter | solution.py:318
  299.0 48.0 %reduce-scatter.27.cloned.1.call-done = bf16[192,3072]{1,0:T(8,128)(2,1)} async-done(((bf16[768,3072]{1,0:T(8,128)(2,1)}), bf16[192,3072]{1,0:T(8,128)(2,1)}) %reduce-scatter.27.cloned.1.call-update) | async-done | bytes 1179664 | tf_op jit(solution)/shard_map/reduce_scatter | solution.py:315
  349.8 9.5 %add_convert_fusion = bf16[2,256,768]{2,1,0:T(8,128)(2,1)} fusion(f32[2,256,768]{2,1,0:T(8,128)} %copy-done.7, bf16[3072,768]{1,0:T(8,128)(2,1)} %param.27, f32[768]{0:T(1024)} %param.28, f32[2,256,3072]{2,1,0:T(8,128)} %copy-done.38, f32[3072]{0:T(1024)} %param.26), kind=kOutput, calls=%fused_computation.67 | convolution fusion | flops 2432827392 | bytes 13384704 | tf_op jit(solution)/shard_map/rsf,fd->rsd/dot_general | solution.py:242
  359.2 52.8 %reduce-scatter.33.cloned.1.call-done = bf16[96,192]{1,0:T(8,128)(2,1)} async-done(((bf16[768,192]{1,0:T(8,128)(2,1)}), bf16[96,192]{1,0:T(8,128)(2,1)}) %reduce-scatter.33.cloned.1.call-update) | async-done | bytes 36880
  415.0 39.2 %reduce-scatter.23.cloned.1.call-done = bf16[192,2304]{1,0:T(8,128)(2,1)} async-done(((bf16[768,2304]{1,0:T(8,128)(2,1)}), bf16[192,2304]{1,0:T(8,128)(2,1)}) %reduce-scatter.23.cloned.1.call-update) | async-done | bytes 884752 | tf_op jit(solution)/shard_map/reduce_scatter | solution.py:309
  456.6 5.0 fusion.103
  466.7 41.2 %all-reduce = (f32[5,768]{1,0:T(8,128)}, f32[768]{0:T(1024)}, f32[768]{0:T(1024)}, f32[768]{0:T(1024)}, f32[768]{0:T(1024)}, /*index=5*/f32[3072]{0:T(1024)}, f32[768]{0:T(1024)}) all-reduce(f32[5,768]{1,0:T(8,128)} %convolution_bitcast_fusion, f32[768]{0:T(1024)} %get-tuple-element.424, ...), channel_id=1, replica_groups=mesh['seq'=4,'batch'=8] {'seq','batch'}, use_global_device_ids=true, to_apply=%region_14.15 | all-reduce | flops 10752 | bytes 86016 | tf_op jit(solution)/shard_map/psum | solution.py:336
  507.9 13.7 %reduce-scatter.37.cloned.1.call-done = bf16[96,768]{1,0:T(8,128)(2,1)} async-done(((bf16[768,768]{1,0:T(8,128)(2,1)}), bf16[96,768]{1,0:T(8,128)(2,1)}) %reduce-scatter.37.cloned.1.call-update) | async-done | bytes 147472
  525.1 63.8 %reduce-scatter.35.cloned.1.call-done = bf16[384,192]{1,0:T(8,128)(2,1)} async-done(((bf16[3072,192]{1,0:T(8,128)(2,1)}), bf16[384,192]{1,0:T(8,128)(2,1)}) %reduce-scatter.35.cloned.1.call-update) | async-done | bytes 147472
  592.2 63.3 %reduce-scatter.31.cloned.1.call-done = bf16[288,192]{1,0:T(8,128)(2,1)} async-done(((bf16[2304,192]{1,0:T(8,128)(2,1)}), bf16[288,192]{1,0:T(8,128)(2,1)}) %reduce-scatter.31.cloned.1.call-update) | async-done | bytes 110608
  (188 shorter events, 117.5 us)
Async XLA Ops:
  7.2 39.0 %all-gather.3.cloned.1.call-start = ((), (), s32[]{:S(2)}) async-start(), calls=%async_computation.10 | async-start | bytes 3932160 | tf_op jit(solution)/shard_map/all_gather | solution.py:204
  12.9 6.0 copy-start.34
  14.8 62.1 %all-gather.5.cloned.1.call-start = ((), (), s32[]{:S(2)}) async-start(), calls=%async_computation.11 | async-start | bytes 3932160 | tf_op jit(solution)/shard_map/all_gather | solution.py:205
  15.6 211.1 %reduce-scatter.25.cloned.1.call-start = ((), (), s32[]{:S(2)}) async-start(), calls=%async_computation.15 | async-start | bytes 1474560 | tf_op jit(solution)/shard_map/reduce_scatter | solution.py:312
  59.5 4.5 copy-start.4
  59.5 4.7 copy-start.22
  59.6 4.7 copy-start.17
  61.9 10.1 %copy-start.3 = (f32[12,256,1024]{2,1,0:T(8,128)}, f32[12,256,1024]{2,1,0:T(8,128)S(1)}, u32[]{:S(2)}) copy-start(f32[12,256,1024]{2,1,0:T(8,128)S(1)} %get-tuple-element.474) | copy-start | bytes 37748740
  105.7 8.4 %slice-start.2 = ((s8[4718592]{0:T(1024)(128)(4,1)}), s8[4194304]{0:T(1024)(128)(4,1)S(1)}, s32[]{:S(2)}) async-start(s8[4718592]{0:T(1024)(128)(4,1)} %bitcast.192), calls=%async_computation.24 | async-start | bytes 8388608
  108.7 16.2 %copy-start.7 = (f32[2,256,768]{2,1,0:T(8,128)}, f32[2,256,768]{2,1,0:T(8,128)S(1)}, u32[]{:S(2)}) copy-start(f32[2,256,768]{2,1,0:T(8,128)S(1)} %get-tuple-element.478) | copy-start | bytes 4718596
  109.1 5.0 copy-start.14
  109.1 5.0 slice-start.3
  109.1 5.0 copy-start.35
  109.1 12.2 %slice-start = ((s8[4718592]{0:T(1024)(128)(4,1)}), s8[4194304]{0:T(1024)(128)(4,1)S(1)}, s32[]{:S(2)}) async-start(s8[4718592]{0:T(1024)(128)(4,1)} %bitcast.190), calls=%async_computation.22 | async-start | bytes 8388608
  114.1 7.2 %copy-start.38 = (f32[2,256,3072]{2,1,0:T(8,128)}, f32[2,256,3072]{2,1,0:T(8,128)S(1)}, u32[]{:S(2)}) copy-start(f32[2,256,3072]{2,1,0:T(8,128)S(1)} %fusion.33) | copy-start | bytes 18874372
  114.1 7.2 %slice-start.1 = ((s8[4718592]{0:T(1024)(128)(4,1)}), s8[524288]{0:T(1024)(128)(4,1)S(1)}, s32[]{:S(2)}) async-start(s8[4718592]{0:T(1024)(128)(4,1)} %bitcast.190), calls=%async_computation.23 | async-start | bytes 1048576
  133.0 105.6 %reduce-scatter.21.cloned.1.call-start = ((), (), s32[]{:S(2)}) async-start(), calls=%async_computation.13 | async-start | bytes 3932160 | tf_op jit(solution)/shard_map/reduce_scatter | solution.py:289
  167.5 78.6 %reduce-scatter.19.cloned.1.call-start = ((), (), s32[]{:S(2)}) async-start(), calls=%async_computation.12 | async-start | bytes 3932160 | tf_op jit(solution)/shard_map/reduce_scatter | solution.py:286
  169.1 8.8 %copy-start.13 = (bf16[1,256,768]{1,2,0:T(8,128)(2,1)S(1)}, bf16[1,256,768]{1,2,0:T(8,128)(2,1)}, u32[]{:S(2)}) copy-start(bf16[1,256,768]{1,2,0:T(8,128)(2,1)} %copy.81) | copy-start | bytes 1179652
  185.0 9.1 %copy-start.12 = (bf16[1,256,768]{1,2,0:T(8,128)(2,1)S(1)}, bf16[1,256,768]{1,2,0:T(8,128)(2,1)}, u32[]{:S(2)}) copy-start(bf16[1,256,768]{1,2,0:T(8,128)(2,1)} %copy.78) | copy-start | bytes 1179652
  203.7 92.8 %reduce-scatter.29.cloned.1.call-start = ((), (), s32[]{:S(2)}) async-start(), calls=%async_computation.17 | async-start | bytes 5898240 | tf_op jit(solution)/shard_map/reduce_scatter | solution.py:318
  212.7 134.2 %reduce-scatter.27.cloned.1.call-start = ((), (), s32[]{:S(2)}) async-start(), calls=%async_computation.16 | async-start | bytes 5898240 | tf_op jit(solution)/shard_map/reduce_scatter | solution.py:315
  220.6 191.4 %reduce-scatter.33.cloned.1.call-start = ((), (), s32[]{:S(2)}) async-start(), calls=%async_computation.19 | async-start | bytes 442368
  228.6 17.6 %copy-start.24 = (f32[2,256]{1,0:T(2,128)S(1)}, f32[2,256]{1,0:T(2,128)}, u32[]{:S(2)}) copy-start(f32[2,256]{1,0:T(2,128)} %copy-done.23) | copy-start | bytes 6148
  228.6 17.5 %copy-start.28 = (f32[2,256]{1,0:T(2,128)S(1)}, f32[2,256]{1,0:T(2,128)}, u32[]{:S(2)}) copy-start(f32[2,256]{1,0:T(2,128)} %copy-done.27) | copy-start | bytes 6148
  228.6 17.5 %copy-start.32 = (f32[768]{0:T(1024)S(1)}, f32[768]{0:T(1024)}, u32[]{:S(2)}) copy-start(f32[768]{0:T(1024)} %param.19) | copy-start | bytes 9220
  228.6 225.6 %reduce-scatter.23.cloned.1.call-start = ((), (), s32[]{:S(2)}) async-start(), calls=%async_computation.14 | async-start | bytes 4423680 | tf_op jit(solution)/shard_map/reduce_scatter | solution.py:309
  252.3 269.3 %reduce-scatter.37.cloned.1.call-start = ((), (), s32[]{:S(2)}) async-start(), calls=%async_computation.21 | async-start | bytes 1327104
  299.0 289.9 %reduce-scatter.35.cloned.1.call-start = ((), (), s32[]{:S(2)}) async-start(), calls=%async_computation.20 | async-start | bytes 1769472
  349.5 306.0 %reduce-scatter.31.cloned.1.call-start = ((), (), s32[]{:S(2)}) async-start(), calls=%async_computation.18 | async-start | bytes 1327104
  456.6 5.0 copy-start.30
  456.6 5.0 copy-start.6
  (24 other events, 67.3 us)
Sparse Core Ops, SparseCore 0:
  15.0 31.2 all-gather.2
  48.4 28.5 all-gather.4
  133.1 25.7 reduce-scatter.24
  167.7 38.0 reduce-scatter.20
  208.1 37.9 reduce-scatter.18
  248.7 47.7 reduce-scatter.28
  299.1 47.8 reduce-scatter.26
  350.6 61.4 reduce-scatter.32
  414.8 39.4 reduce-scatter.22
  457.5 64.0 reduce-scatter.36
  525.0 63.7 reduce-scatter.34
  592.5 62.9 reduce-scatter.30
where the time goes:
time: 670 us; the launch traced here: 666 us
  waiting for transfers between devices  348 us (52%)
  matrix products  144 us (21%)
  local copies, waits for them, and re-layouts  74.2 us (11%)
  blocking collectives  47.6 us (7%)
  other arithmetic  36.3 us (5%)
  between operations  15.1 us (2%)
    unnamed x16, waiting for transfers between devices  194 us
    reduce_scatter x1, waiting for transfers between devices, local(): lax.psum_scatter(grad_w_up.astype(jnp.bfloat16), 'seq', scatter_dimension...  48 us
    reduce_scatter x1, waiting for transfers between devices, local(): lax.psum_scatter(grad_w_down.astype(jnp.bfloat16), 'seq', scatter_dimensi...  44.2 us
    psum x1, blocking collectives, local(): lax.psum((grad_pass, grad_ln1_gain, grad_ln1_bias, grad_ln2_gain, grad_ln...  41.2 us
    reduce_scatter x1, waiting for transfers between devices, local(): lax.psum_scatter(grad_w_qkv.astype(jnp.bfloat16), 'seq', scatter_dimensio...  39.2 us
    unnamed x97, local copies, waits for them, and re-layouts  24.2 us
    dot_general x2, matrix products, add_grads(): jnp.einsum('hqk,qhd->khd', low_chance, dout_part, preferred_element_type=...  19 us
    dot_general x2, matrix products, grad_pieces(): jnp.einsum('qhd,khd->hqk', dout_part, value_part, preferred_element_type=...  17.9 us
  transfers between devices with their start and end apart: 12, of which 10 were waited for; matrix products, arithmetic and copies ran while one was open for 28% of the time, Pallas kernels for 0%

commit v1 on v0

--- a/solution.py
+++ b/solution.py
@@ -1,6 +1,10 @@
+import functools
+
 import jax
 import jax.numpy as jnp
 from jax import lax
+from jax.experimental import pallas as pl
+from jax.experimental.pallas import tpu as pltpu
 from jax.sharding import PartitionSpec as P
 
 H = 12
@@ -362,9 +366,868 @@
     )
 
 
+NN = (((1,), (0,)), ((), ()))
+NT = (((1,), (1,)), ((), ()))
+TN = (((0,), (0,)), ((), ()))
+vmem_bytes = 60 << 20
+block = 256
+
+
+def dot(left, right, form):
+    return lax.dot_general(left, right, form, preferred_element_type=jnp.float32)
+
+
+def lane_loop(total, width, body):
+    def step(i, carry):
+        body(pl.ds(pl.multiple_of(i * width, width), width))
+        return carry
+
+    lax.fori_loop(0, total // width, step, 0)
+
+
+def attend_kernel(
+    info, b0, b1, b2, b3, emb, vecs, wqkv, ht, at, qt, kt, vt, ot, kept, inv, bias, prow, pcol
+):
+    width, total = ht.shape
+    half = qt.shape[0]
+    core = info[4]
+
+    @pl.when(pl.program_id(0) == 0)
+    def _():
+        for k, ref in enumerate((b0, b1, b2, b3)):
+            place = pl.ds(pl.multiple_of(info[k] * block, block), block)
+            passes = ref[block : block + 16, 0:block].astype(jnp.float32)
+            prow[:, place] = passes[0:8, :]
+            pcol[place, :] = jnp.transpose(passes)[:, 0:8]
+            kind = (lax.broadcasted_iota(jnp.int32, (16, block), 0) % 5).astype(jnp.float32)
+            line = lax.broadcasted_iota(jnp.int32, (16, block), 0)
+            onehot = jnp.where((kind == passes[0:1, :]) & (line < 15), 1.0, 0.0)
+            added = dot(emb[...], onehot.astype(jnp.bfloat16), NN)
+            ht[:, place] = jnp.transpose(ref[0:block, :]).astype(jnp.float32) + added
+
+        def norm(cols):
+            h = ht[:, cols]
+            shifted = h - jnp.sum(h, 0, keepdims=True) * (1.0 / width)
+            spread = jnp.sum(shifted * shifted, 0, keepdims=True) * (1.0 / width)
+            scaled = shifted * lax.rsqrt(spread + 1e-05)
+            at[:, cols] = (scaled * vecs[:, 0:1] + vecs[:, 1:2]).astype(jnp.bfloat16)
+
+        lane_loop(total, 128, norm)
+        for j, (ref, factor) in enumerate(((qt, 0.125), (kt, 1.0), (vt, 1.0))):
+            cols = pl.ds(pl.multiple_of(j * width + core * half, 128), half)
+            part = dot(wqkv[:, cols], at[...], TN).astype(jnp.bfloat16)
+            ref[...] = part if factor == 1.0 else part * jnp.bfloat16(factor)
+        length = info[5]
+        for qb in range(total // block):
+            n = (qb + 1) * block
+            keys = lax.broadcasted_iota(jnp.int32, (n, block), 0)
+            place = lax.broadcasted_iota(jnp.int32, (n, block), 1) + qb * block
+            allowed = (pcol[0:n, 0:1] <= prow[0:1, qb * block : n]) & (keys < length)
+            allowed = (allowed & (keys < place)) | (keys == place)
+            at_row = qb * (qb + 1) // 2 * block
+            bias[at_row : at_row + n, :] = jnp.where(allowed, 0.0, negative)
+
+    head = pl.program_id(0)
+    rows = pl.ds(pl.multiple_of(head * 64, 64), 64)
+    keyn = jnp.transpose(kt[rows, :])
+    for qb in range(total // block):
+        n = (qb + 1) * block
+        at_row = qb * (qb + 1) // 2 * block
+        scores = dot(keyn[0:n, :], qt[rows, qb * block : n], NN) + bias[at_row : at_row + n, :]
+        peak = jnp.max(scores, 0, keepdims=True)
+        expo = jnp.exp(scores - peak)
+        over = 1.0 / jnp.sum(expo, 0, keepdims=True)
+        low = expo.astype(jnp.bfloat16)
+        kept[0, at_row : at_row + n, :] = low
+        inv[0, :, qb * block : n] = jnp.broadcast_to(over, (8, block))
+        result = dot(vt[rows, 0:n], low, NN) * over
+        ot[rows, qb * block : n] = result.astype(jnp.bfloat16)
+
+
+mesh_ids = pl.DeviceIdType.MESH
+
+
+def prepare_kernel(info, w_up, w_up_t):
+    width, inner = w_up.shape
+    bands = 8
+    band = inner // bands
+    for b in range(bands):
+        turned = jnp.transpose(w_up[:, b * band : (b + 1) * band])
+        w_up_t[b * band // 2 : (b + 1) * band // 2, :] = jnp.where(
+            info[4] == 0, turned[: band // 2], turned[band // 2 :]
+        )
+
+
+def turn_kernel(info, c0, c1, c2, c3, ct):
+    for k, ref in enumerate((c0, c1, c2, c3)):
+        place = pl.ds(pl.multiple_of(info[k] * block, block), block)
+        ct[:, place] = jnp.transpose(ref[...])
+
+
+def back_kernel(
+    ot_own, ot_recv, ht_in, at_in, qt_in, kt_in, vt_in, kept_in, ct_in,
+    w_out_in, w_qkv_in, w_up_in, w_down_in,
+    inv, prow, b_up, vecs,
+    out, gin, vector, gqkv, gout, gup, gdown,
+    mid, keep, at, qkv, otf, ct, mt, gd, far, dm, kept, w_out, w_up, w_down,
+    bsum, r1a, r2a, r1c, r2c, rz, osend, orecv, hand, sums, gpass, vrecv, ksum, vsum,
+    stage_send, stage_recv, down_recv,
+    lsem, ssem, rsem,
+    *, chunks, plan, rest_plan,
+):
+    seq, bat = lax.axis_index("seq"), lax.axis_index("batch")
+    x, core = seq // 2, seq % 2
+    z, y = bat // 2, bat % 2
+    to_core, to_x, to_y = (seq + 1 - 2 * core, bat), (seq + 2 - 4 * x, bat), (seq, bat + 1 - 2 * y)
+    to_z = [(seq, ((z + i) % 4) * 2 + y) for i in (1, 2, 3)]
+    up_z, low_z = (seq, bat + 2), (seq, bat - 2)
+
+    barrier = pltpu.get_barrier_semaphore()
+    for peer in [to_core, to_x, to_y] + to_z:
+        pl.semaphore_signal(barrier, inc=1, device_id=peer, device_id_type=mesh_ids)
+
+    width, total = mid.shape
+    half = width // 2
+    inner = w_up.shape[0]
+    blocks_n = total // block
+    heads = kept_in.shape[0]
+
+    def rows_at(first, count):
+        return pl.ds(pl.multiple_of(first, 16), count)
+
+    def local(i, src, dst):
+        return pltpu.make_async_copy(src, dst, lsem.at[i])
+
+    loads = {
+        "o1": local(0, ot_own, otf.at[rows_at(core * half, half), :]),
+        "o2": local(1, ot_recv, otf.at[rows_at((1 - core) * half, half), :]),
+        "w_out": local(2, w_out_in, w_out),
+        "h": local(3, ht_in, mid),
+        "w_up": local(4, w_up_in, w_up),
+        "ct": local(5, ct_in, ct),
+        "at": local(7, at_in, at),
+        "q": local(8, qt_in, qkv.at[0:half, :]),
+        "k": local(9, kt_in, qkv.at[half : 2 * half, :]),
+        "v": local(10, vt_in, qkv.at[2 * half : 3 * half, :]),
+    }
+    part = w_down_in.shape[2]
+    for i in range(w_down_in.shape[0]):
+        loads["w_down%d" % i] = local(
+            18 + i, w_down_in.at[i, core], w_down.at[i * part : (i + 1) * part, :]
+        )
+    for load in loads.values():
+        load.start()
+
+    def kept_load(h, slot):
+        return pltpu.make_async_copy(kept_in.at[h], kept.at[slot], lsem.at[11 + slot])
+
+    kept_load(0, 0).start()
+    kept_load(1, 1).start()
+
+    def remote(i, src, dst, peer):
+        return pltpu.make_async_remote_copy(
+            src_ref=src, dst_ref=dst, send_sem=ssem.at[i], recv_sem=rsem.at[i],
+            device_id=peer, device_id_type=mesh_ids,
+        )
+
+    def first(k):
+        r0, ra, r1, a0, c0 = chunks[k]
+        na, nc = ra - r0, r1 - ra
+        return (
+            remote(12 * k, bsum.at[1 - x, :, :, r0:ra, :], r1a.at[:, :, a0 : a0 + na, :], to_x),
+            remote(
+                12 * k + 1, bsum.at[:, :, 1 - y, ra:r1, :], r1c.at[:, :, c0 : c0 + nc, :], to_y
+            ),
+        )
+
+    def second(k):
+        r0, ra, r1, a0, c0 = chunks[k]
+        na, nc = ra - r0, r1 - ra
+        return (
+            remote(12 * k + 2, bsum.at[x, :, 1 - y, r0:ra, :], r2a.at[:, a0 : a0 + na, :], to_y),
+            remote(12 * k + 3, bsum.at[1 - x, :, y, ra:r1, :], r2c.at[:, c0 : c0 + nc, :], to_x),
+        )
+
+    def up_copy(k, d):
+        r0, _, r1, _, _ = chunks[k]
+        return remote(12 * k + 4 + d, bsum.at[x, d, y, r0:r1, :], rz.at[d, r0:r1, :], up_z)
+
+    def low_copy(k, d):
+        r0, _, r1, _, _ = chunks[k]
+        slot = jnp.where(z - 1 == d, 4, d)
+        return remote(12 * k + 8 + d, bsum.at[x, d, y, r0:r1, :], rz.at[slot, r0:r1, :], low_z)
+
+    def add_z(k, d, slot):
+        r0, _, r1, _, _ = chunks[k]
+        bsum[x, d, y, r0:r1, :] = bsum[x, d, y, r0:r1, :] + rz[slot, r0:r1, :]
+
+    def step_start(k):
+        for copy in first(k):
+            copy.start()
+
+    def step_second(k):
+        r0, ra, r1, a0, c0 = chunks[k]
+        na, nc = ra - r0, r1 - ra
+        one, two = first(k)
+        three, four = second(k)
+        one.wait()
+        bsum[x, :, :, r0:ra, :] = bsum[x, :, :, r0:ra, :] + r1a[:, :, a0 : a0 + na, :]
+        three.start()
+        two.wait()
+        bsum[:, :, y, ra:r1, :] = bsum[:, :, y, ra:r1, :] + r1c[:, :, c0 : c0 + nc, :]
+        four.start()
+
+    def step_line(k):
+        r0, ra, r1, a0, c0 = chunks[k]
+        na, nc = ra - r0, r1 - ra
+        three, four = second(k)
+        three.wait()
+        bsum[x, :, y, r0:ra, :] = bsum[x, :, y, r0:ra, :] + r2a[:, a0 : a0 + na, :]
+        four.wait()
+        bsum[x, :, y, ra:r1, :] = bsum[x, :, y, ra:r1, :] + r2c[:, c0 : c0 + nc, :]
+
+        @pl.when(z == 0)
+        def _():
+            for d in (3, 2, 1):
+                up_copy(k, d).start()
+
+        @pl.when(z == 3)
+        def _():
+            for d in (0, 1, 2):
+                low_copy(k, d).start()
+
+    def pass_up(k, d):
+        up_copy(k, d).wait_recv()
+        add_z(k, d, d)
+        up_copy(k, d).start()
+
+    def pass_low(k, d):
+        low_copy(k, d).wait_recv()
+        add_z(k, d, d)
+        low_copy(k, d).start()
+
+    def step_pass(k):
+        @pl.when(z == 1)
+        def _():
+            pass_up(k, 3)
+
+        @pl.when(z == 2)
+        def _():
+            pass_low(k, 0)
+
+    def step_pass_more(k):
+        @pl.when(z == 1)
+        def _():
+            pass_up(k, 2)
+            pass_low(k, 0)
+
+        @pl.when(z == 2)
+        def _():
+            pass_low(k, 1)
+            pass_up(k, 3)
+
+    def step_last(k):
+        for d in range(4):
+
+            @pl.when(z == d)
+            def _():
+                if d > 0:
+                    up_copy(k, d).wait_recv()
+                    add_z(k, d, d)
+                if d < 3:
+                    low_copy(k, d).wait_recv()
+                    add_z(k, d, 4)
+                for e in range(4):
+                    if e > d:
+                        up_copy(k, e).wait_send()
+                    if e < d:
+                        low_copy(k, e).wait_send()
+
+    steps = (step_start, step_second, step_line, step_pass, step_pass_more, step_last)
+
+    loads["o1"].wait()
+    loads["o2"].wait()
+    loads["w_out"].wait()
+    loads["h"].wait()
+
+    def mix(i, carry):
+        cols = pl.ds(pl.multiple_of(i * block, block), block)
+        m = mid[:, cols] + dot(w_out[...], otf[:, cols], TN)
+        mid[:, cols] = m
+        shifted = m - jnp.sum(m, 0, keepdims=True) * (1.0 / width)
+        spread = jnp.sum(shifted * shifted, 0, keepdims=True) * (1.0 / width)
+        scaled = shifted * lax.rsqrt(spread + 1e-05)
+        mt[:, cols] = (scaled * vecs[:, 2:3] + vecs[:, 3:4]).astype(jnp.bfloat16)
+        return carry
+
+    lax.fori_loop(0, blocks_n, mix, 0)
+    loads["w_up"].wait()
+    loads["ct"].wait()
+    for i in range(w_down_in.shape[0]):
+        loads["w_down%d" % i].wait()
+
+    def hidden(i, carry):
+        rows = pl.ds(pl.multiple_of(i * part, part), part)
+        below = pl.ds(pl.multiple_of(inner + i * part, part), part)
+        u = dot(w_up[rows, :], mt[...], NN) + b_up[rows, 0:1]
+        back = dot(w_down[rows, :], ct[...], NN)
+        square = u * u
+        t = jnp.tanh(u * (0.7978845608028654 + 0.035677408136300125 * square))
+        gate = 0.5 + 0.5 * t
+        gd[rows, :] = (u * gate).astype(jnp.bfloat16)
+        slope = gate + (0.5 * u) * (1.0 - t * t) * (
+            0.7978845608028654 + 0.10703222440890037 * square
+        )
+        gd[below, :] = (back * slope).astype(jnp.bfloat16)
+        return carry
+
+    lax.fori_loop(0, inner // part, hidden, 0)
+    lanes = bsum.shape[-1]
+    bs = 8
+    band = width // bs
+    for xx in range(2):
+        for j in range(2):
+            at_row = (2 * xx + j) * lanes
+            grad = dot(ct[...], gd[at_row : at_row + lanes, :], NT).astype(jnp.bfloat16)
+            for b in range(bs):
+                bsum[xx, b // 2, b % 2, j * band : (j + 1) * band, :] = grad[
+                    b * band : (b + 1) * band, :
+                ]
+    pl.semaphore_wait(barrier, 6)
+    steps[0](0)
+
+    base = 12 * len(chunks)
+    dm_copy = remote(base, dm.at[0:width, :], dm.at[width : 2 * width, :], to_core)
+
+    def back_up(i, carry):
+        cols = pl.ds(pl.multiple_of(i * block, block), block)
+        dm[0:width, cols] = dot(w_up[...], gd[inner : 2 * inner, cols], TN).astype(jnp.bfloat16)
+        return carry
+
+    lax.fori_loop(0, blocks_n, back_up, 0)
+    dm_copy.start()
+    first_up = 2 * band
+    up_band = part
+    for xx in range(2):
+        for i in range(2):
+            low, high = inner + i * inner // 2, inner + (i + 1) * inner // 2
+            grad = dot(gd[low:high, :], mt[xx * lanes : (xx + 1) * lanes, :], NT)
+            grad = grad.astype(jnp.bfloat16)
+            for b in range(bs // 2):
+                bb = i * bs // 2 + b
+                bsum[xx, bb // 2, bb % 2, first_up : first_up + up_band, :] = grad[
+                    b * up_band : (b + 1) * up_band, :
+                ]
+    ones = jnp.ones((8, total), jnp.bfloat16)
+    up_sum = dot(ones, gd[inner : 2 * inner, :], NT)
+    vector[...] = jnp.zeros_like(vector)
+    for c in range(2):
+        for i in range(2):
+            line = up_sum[0:1, i * width : (i + 1) * width]
+            vector[10 + 2 * c + i : 11 + 2 * c + i, :] = jnp.where(core == c, line, 0.0)
+    out_copy = remote(base + 1, osend, orecv, to_core)
+    for k in range(2):
+        mine = pl.ds(pl.multiple_of(core * block + k * 2 * block, block), block)
+        other = pl.ds(pl.multiple_of((1 - core) * block + k * 2 * block, block), block)
+        to = slice(k * block, (k + 1) * block)
+        osend[:, to] = dot(w_down[...], gd[0:inner, other], TN).astype(jnp.bfloat16)
+        keep[:, to] = mid[:, mine] + vecs[:, 4:5] + dot(w_down[...], gd[0:inner, mine], TN)
+    out_copy.start()
+
+    dm_copy.wait()
+    sums[...] = jnp.zeros_like(sums)
+
+    def middle(i, carry):
+        cols = pl.ds(pl.multiple_of(i * block, block), block)
+        cot = ct[:, cols].astype(jnp.float32)
+        m = mid[:, cols]
+        shifted = m - jnp.sum(m, 0, keepdims=True) * (1.0 / width)
+        spread = jnp.sum(shifted * shifted, 0, keepdims=True) * (1.0 / width)
+        r = lax.rsqrt(spread + 1e-05)
+        n = shifted * r
+        d = dm[0:width, cols].astype(jnp.float32) + dm[width : 2 * width, cols].astype(jnp.float32)
+        e = d * vecs[:, 2:3]
+        mean_e = jnp.sum(e, 0, keepdims=True) * (1.0 / width)
+        mean_en = jnp.sum(e * n, 0, keepdims=True) * (1.0 / width)
+        dmid = cot + r * (e - mean_e - n * mean_en)
+        mid[:, cols] = dmid
+        dm[width : 2 * width, cols] = dmid.astype(jnp.bfloat16)
+        sums[:, 0:1] += jnp.sum(d * n, 1, keepdims=True)
+        sums[:, 1:2] += jnp.sum(d, 1, keepdims=True)
+        sums[:, 2:3] += jnp.sum(cot, 1, keepdims=True)
+        return carry
+
+    lax.fori_loop(0, blocks_n, middle, 0)
+    small = band // 2
+    for b in range(bs):
+        dm[half + b * small : half + (b + 1) * small, :] = dm[
+            rows_at(width + b * band + core * small, small), :
+        ]
+    first_out = first_up + up_band
+    for xx in range(2):
+        grad = dot(dm[half:width, :], otf[xx * lanes : (xx + 1) * lanes, :], NT)
+        grad = grad.astype(jnp.bfloat16)
+        for b in range(bs):
+            bsum[xx, b // 2, b % 2, first_out : first_out + small, :] = grad[
+                b * small : (b + 1) * small, :
+            ]
+    steps[0](1)
+    dm[0:half, :] = dot(
+        w_out[rows_at(core * half, half), :], dm[width : 2 * width, :], NN
+    ).astype(jnp.bfloat16)
+
+    whole_loads = [
+        local(13, w_qkv_in.at[:, 0:width], w_up.at[0:width, :]),
+        local(14, w_qkv_in.at[:, width : 2 * width], w_up.at[width : 2 * width, :]),
+        local(15, w_qkv_in.at[:, 2 * width : 3 * width], w_down.at[0:width, :]),
+    ]
+    for load in whole_loads:
+        load.start()
+
+    out_copy.wait()
+    hand_out = remote(base + 2, hand.at[0], out.at[x], to_x)
+    for k in range(2):
+        cols = slice(k * block, (k + 1) * block)
+        rows = jnp.transpose(
+            (keep[:, cols] + orecv[:, cols].astype(jnp.float32)).astype(jnp.bfloat16)
+        )
+
+        @pl.when(x == k)
+        def _():
+            out[k] = rows
+
+        @pl.when(x != k)
+        def _():
+            hand[0] = rows
+
+    hand_out.start()
+    own_loads = [
+        local(16 + k, ht_in.at[:, pl.ds(pl.multiple_of(core * block + k * 2 * block, block), block)],
+              keep.at[:, k * block : (k + 1) * block])
+        for k in range(2)
+    ]
+    for load in own_loads:
+        load.start()
+
+    for name in ("at", "q", "k", "v"):
+        loads[name].wait()
+
+    def far_copy(h, j):
+        mine = rows_at(j * width + core * half + h * 64, 64)
+        return remote(
+            base + 3 + h * 3 + j, gd.at[mine, :], far.at[rows_at(j * half + h * 64, 64), :], to_core
+        )
+
+    def one_head(h, carry):
+        slot = h % 2
+        kept_load(h, slot).wait()
+        qrow, krow, vrow = (rows_at(j * half + h * 64, 64) for j in range(3))
+        mine = [rows_at(j * width + core * half + h * 64, 64) for j in range(3)]
+        valn = jnp.transpose(qkv[vrow, :])
+        grads = (dm[rows_at(h * 64, 64), :].astype(jnp.float32) * inv[h, 0:1, :]).astype(
+            jnp.bfloat16
+        )
+        o_rows = otf[rows_at(core * half + h * 64, 64), :]
+        delta = jnp.sum(grads.astype(jnp.float32) * o_rows.astype(jnp.float32), 0, keepdims=True)
+        ksum[...] = jnp.zeros_like(ksum)
+        vsum[...] = jnp.zeros_like(vsum)
+        for qb in range(blocks_n):
+            n = (qb + 1) * block
+            at_row = qb * (qb + 1) // 2 * block
+            cols = slice(qb * block, n)
+            low = kept[slot, at_row : at_row + n, :]
+            dprob = dot(valn[0:n, :], grads[:, cols], NN)
+            dscore = (low.astype(jnp.float32) * (dprob - delta[:, cols])).astype(jnp.bfloat16)
+            gd[mine[0], cols] = (dot(qkv[krow, 0:n], dscore, NN) * 0.125).astype(jnp.bfloat16)
+            ksum[:, 0:n] += dot(qkv[qrow, cols], dscore, NT)
+            vsum[:, 0:n] += dot(grads[:, cols], low, NT)
+        gd[mine[1], :] = ksum[...].astype(jnp.bfloat16)
+        gd[mine[2], :] = vsum[...].astype(jnp.bfloat16)
+        for j in range(3):
+            far_copy(h, j).start()
+
+        @pl.when(h + 2 < heads)
+        def _():
+            kept_load(h + 2, slot).start()
+
+        for at_head, which, k in plan:
+
+            @pl.when(h == at_head)
+            def _():
+                steps[which](k)
+
+        return carry
+
+    lax.fori_loop(0, heads, one_head, 0)
+
+    for h in range(heads):
+        for j in range(3):
+            far_copy(h, j).wait()
+    for j in range(3):
+        gd[rows_at(j * width + (1 - core) * half, half), :] = far[j * half : (j + 1) * half, :]
+    qkv_band = 3 * width // bs
+    qkv_small = qkv_band // 2
+    for b in range(bs):
+        dm[b * qkv_small : (b + 1) * qkv_small, :] = gd[
+            rows_at(b * qkv_band + core * qkv_small, qkv_small), :
+        ]
+    first_qkv = first_out + small
+    for xx in range(2):
+        grad = dot(dm[0 : bs * qkv_small, :], at[xx * lanes : (xx + 1) * lanes, :], NT)
+        grad = grad.astype(jnp.bfloat16)
+        for b in range(bs):
+            bsum[xx, b // 2, b % 2, first_qkv : first_qkv + qkv_small, :] = grad[
+                b * qkv_small : (b + 1) * qkv_small, :
+            ]
+    steps[0](2)
+
+    for load in whole_loads + own_loads:
+        load.wait()
+    gpass[...] = jnp.zeros_like(gpass)
+    hand_in = remote(base + 21, hand.at[1], gin.at[x], to_x)
+    for k in range(2):
+        mine = pl.ds(pl.multiple_of(core * block + k * 2 * block, block), block)
+        da = dot(w_up[0:width, :], gd[0:width, mine], NN)
+        da += dot(w_up[width : 2 * width, :], gd[width : 2 * width, mine], NN)
+        da += dot(w_down[0:width, :], gd[2 * width : 3 * width, mine], NN)
+        h = keep[:, k * block : (k + 1) * block]
+        shifted = h - jnp.sum(h, 0, keepdims=True) * (1.0 / width)
+        spread = jnp.sum(shifted * shifted, 0, keepdims=True) * (1.0 / width)
+        r = lax.rsqrt(spread + 1e-05)
+        n = shifted * r
+        e = da * vecs[:, 0:1]
+        mean_e = jnp.sum(e, 0, keepdims=True) * (1.0 / width)
+        mean_en = jnp.sum(e * n, 0, keepdims=True) * (1.0 / width)
+        dh = mid[:, mine] + r * (e - mean_e - n * mean_en)
+        rows = jnp.transpose(dh).astype(jnp.bfloat16)
+
+        @pl.when(x == k)
+        def _():
+            gin[k] = rows
+
+        @pl.when(x != k)
+        def _():
+            hand[1] = rows
+            hand_in.start()
+
+        sums[:, 3:4] += jnp.sum(da * n, 1, keepdims=True)
+        sums[:, 4:5] += jnp.sum(da, 1, keepdims=True)
+        kind = lax.broadcasted_iota(jnp.int32, (16, block), 0).astype(jnp.float32)
+        onehot = jnp.where(kind == prow[0:1, mine], 1.0, 0.0).astype(jnp.bfloat16)
+        high = dh.astype(jnp.bfloat16)
+        rest = dh - high.astype(jnp.float32)
+        second_part = rest.astype(jnp.bfloat16)
+        tail = (rest - second_part.astype(jnp.float32)).astype(jnp.bfloat16)
+        gpass[...] += dot(onehot, high, NT) + dot(onehot, second_part, NT) + dot(onehot, tail, NT)
+
+    lines = jnp.transpose(sums[...])
+    vector[0:5, :] = gpass[0:5, :]
+    vector[5:7, :] = lines[3:5, :]
+    vector[7:10, :] = lines[0:3, :] * 0.5
+    for i, peer in enumerate((to_core, to_x, to_y)):
+        copy = remote(base + 22 + i, vector, vrecv.at[i], peer)
+        copy.start()
+        copy.wait()
+        vector[...] = vector[...] + vrecv[i]
+        for which, k in rest_plan[i]:
+            steps[which](k)
+    copies = [
+        remote(base + 25 + i, vector, vrecv.at[3 + z], peer) for i, peer in enumerate(to_z)
+    ]
+    for copy in copies:
+        copy.start()
+    vrecv[3 + z] = vector[...]
+
+    own_rows = down_recv.shape[0]
+    down_copy = remote(
+        base + 28, bsum.at[x, z, y, rows_at((1 - core) * own_rows, own_rows), :], down_recv, to_core
+    )
+
+    def swap_lanes(i, r0, r1):
+        wide = lanes // 2
+        v = bsum[x, z, y, r0:r1, :]
+        stage_send[r0 - first_up : r1 - first_up, 0:wide] = jnp.where(
+            core == 0, v[:, wide:lanes], v[:, 0:wide]
+        )
+        at_rows = slice(r0 - first_up, r1 - first_up)
+        return remote(base + i, stage_send.at[at_rows, :], stage_recv.at[at_rows, :], to_core)
+
+    def both_cores(mine, got):
+        return jnp.where(core == 0, mine, got), jnp.where(core == 0, got, mine)
+
+    def put(result, r0, r1):
+        wide = lanes // 2
+        v = bsum[x, z, y, r0:r1, :].astype(jnp.float32)
+        mine = jnp.where(core == 0, v[:, 0:wide], v[:, wide:lanes])
+        got = stage_recv[r0 - first_up : r1 - first_up, 0:wide].astype(jnp.float32)
+        result[...] = jnp.transpose(jnp.concatenate(both_cores(mine, got), 0))
+
+    swaps = []
+    for which, k in rest_plan[3]:
+        steps[which](k)
+        if which == 5:
+            if k == 0:
+                swaps.append(down_copy)
+            else:
+                swaps.append(swap_lanes(28 + k, chunks[k][0], chunks[k][2]))
+            swaps[-1].start()
+    swaps[0].wait()
+    mine = bsum[x, z, y, rows_at(core * own_rows, own_rows), :].astype(jnp.float32)
+    for c, piece in enumerate(both_cores(mine, down_recv[...].astype(jnp.float32))):
+        turned = jnp.transpose(piece)
+        for i in range(lanes // part):
+            at_row = (2 * i + c) * part
+            gdown[at_row : at_row + part, :] = turned[i * part : (i + 1) * part, :]
+    swaps[1].wait()
+    put(gup, first_up, first_out)
+    put(gout, first_out, first_qkv)
+    for copy in copies:
+        copy.wait()
+    vector[...] = (vrecv[3] + vrecv[4]) + (vrecv[5] + vrecv[6])
+    hand_out.wait()
+    hand_in.wait()
+    swaps[2].wait()
+    put(gqkv, first_qkv, first_qkv + qkv_small)
+
+
+def call(kernel, outs, scratch=(), smem=True, n_in=0, name=None, flops=0, **kw):
+    in_specs = [pl.BlockSpec(memory_space=pltpu.VMEM)] * n_in
+    if smem:
+        in_specs[0] = pl.BlockSpec(memory_space=pltpu.SMEM)
+    return pl.pallas_call(
+        kernel,
+        out_shape=outs,
+        in_specs=in_specs,
+        out_specs=[pl.BlockSpec(memory_space=pltpu.VMEM)] * len(outs),
+        scratch_shapes=list(scratch),
+        compiler_params=pltpu.CompilerParams(vmem_limit_bytes=vmem_bytes),
+        cost_estimate=pl.CostEstimate(flops=int(flops), bytes_accessed=0, transcendentals=0),
+        name=name,
+        **kw,
+    )
+
+
+def shaped(*dims, kind=jnp.bfloat16):
+    return jax.ShapeDtypeStruct(dims, kind)
+
+
+def pick(array, axis, index):
+    return lax.dynamic_index_in_dim(array, index, axis, keepdims=False)
+
+
+def swap(array, axis, size, distance):
+    return lax.ppermute(array, axis, [(i, i ^ distance) for i in range(size)])
+
+
+def regrouped(
+    block_input, lengths, pass_ids, pass_embed, ln1_gain, ln1_bias, w_qkv, w_out,
+    ln2_gain, ln2_bias, w_up, b_up, w_down, b_down, cotangent, batch_n, y_n
+):
+    row_count, seg_len, width = block_input.shape
+    total = 4 * seg_len
+    inner = w_up.shape[1]
+    own_in = inner // 2
+    heads_own = H // 2
+    half = width // 2
+    z_n = batch_n // y_n
+    s = lax.axis_index("seq")
+    x, core = s // 2, s % 2
+    bat = lax.axis_index("batch")
+    z, y = bat // y_n, bat % y_n
+
+    def by_x(array):
+        return swap(array, "seq", 4, 2)
+
+    def by_core(array):
+        return swap(array, "seq", 4, 1)
+
+    def by_y(array):
+        return swap(array, "batch", batch_n, 1)
+
+    pass_rows = jnp.zeros((row_count, 16, width), jnp.bfloat16)
+    pass_rows = lax.dynamic_update_slice(
+        pass_rows,
+        jnp.broadcast_to(pass_ids.astype(jnp.bfloat16)[:, None, :], (row_count, 16, seg_len)),
+        (0, 0, 0),
+    )
+    packed = jnp.concatenate([block_input, pass_rows], 1)
+    x_own = pick(packed, 0, x)
+    x_far = by_x(pick(packed, 0, 1 - x))
+    x_near = by_core(x_own)
+    x_cross = by_core(x_far)
+    c_own = pick(cotangent, 0, x)
+    c_far = by_x(pick(cotangent, 0, 1 - x))
+    c_near = by_core(c_own)
+    c_cross = by_core(c_far)
+    length = pick(lengths, 0, x)
+    info = jnp.stack(
+        [2 * x + core, 2 * (1 - x) + core, 2 * x + 1 - core, 2 * (1 - x) + 1 - core, core, length]
+    ).astype(jnp.int32)
+
+    embed_t = jnp.transpose(pass_embed)
+    first = embed_t.astype(jnp.bfloat16)
+    rest = embed_t - first.astype(jnp.float32)
+    second = rest.astype(jnp.bfloat16)
+    third = (rest - second.astype(jnp.float32)).astype(jnp.bfloat16)
+    emb = jnp.concatenate([first, second, third, jnp.zeros((width, 1), jnp.bfloat16)], 1)
+    zero = jnp.zeros_like(ln1_gain)
+    vecs = jnp.stack([ln1_gain, ln1_bias, ln2_gain, ln2_bias, b_down, zero, zero, zero], 1)
+    band = inner // batch_n // 2
+    (w_up_t,) = call(
+        prepare_kernel, [shaped(own_in, width)], n_in=2, name="prepare", flops=2e9
+    )(info, w_up)
+    w_down_parts = w_down.reshape(batch_n, 2, band, width)
+    b_up_own = pick(b_up.reshape(batch_n, 2, band), 1, core).reshape(own_in, 1)
+    b_up_own = jnp.broadcast_to(b_up_own, (own_in, 8))
+
+    blocks_n = total // block
+    kept_rows = blocks_n * (blocks_n + 1) // 2 * block
+    whole = pl.BlockSpec(memory_space=pltpu.VMEM)
+
+    def fixed(*dims):
+        return pl.BlockSpec(dims, lambda i: (0,) * len(dims))
+
+    ht, at, qt, kt, vt, ot, kept, inv, prow = pl.pallas_call(
+        lambda *refs: attend_kernel(*refs[:8], *refs[8:16], refs[17], refs[16], refs[18]),
+        out_shape=[
+            shaped(width, total, kind=jnp.float32),
+            shaped(width, total),
+            shaped(half, total),
+            shaped(half, total),
+            shaped(half, total),
+            shaped(half, total),
+            shaped(heads_own, kept_rows, block),
+            shaped(heads_own, 8, total, kind=jnp.float32),
+            shaped(8, total, kind=jnp.float32),
+        ],
+        grid=(heads_own,),
+        in_specs=[pl.BlockSpec(memory_space=pltpu.SMEM)]
+        + [fixed(seg_len + 16, width)] * 4
+        + [fixed(width, 16), fixed(width, 8), fixed(width, 3 * width)],
+        out_specs=[
+            fixed(width, total),
+            fixed(width, total),
+            fixed(half, total),
+            fixed(half, total),
+            fixed(half, total),
+            fixed(half, total),
+            pl.BlockSpec((1, kept_rows, block), lambda i: (i, 0, 0)),
+            pl.BlockSpec((1, 8, total), lambda i: (i, 0, 0)),
+            fixed(8, total),
+        ],
+        scratch_shapes=[
+            pltpu.VMEM((kept_rows, block), jnp.float32),
+            pltpu.VMEM((total, 8), jnp.float32),
+        ],
+        compiler_params=pltpu.CompilerParams(vmem_limit_bytes=vmem_bytes),
+        cost_estimate=pl.CostEstimate(flops=int(12e9), bytes_accessed=0, transcendentals=0),
+        name="attend",
+    )(info, x_own, x_far, x_near, x_cross, emb, vecs, w_qkv)
+
+    ot_recv = by_core(ot)
+    (ct,) = call(turn_kernel, [shaped(width, total)], n_in=5, name="turn", flops=1e9)(
+        info, c_own, c_far, c_near, c_cross
+    )
+    lanes = width // 2
+    down_n, up_n, out_n, qkv_n = 2 * width // batch_n, band, width // batch_n // 2, 3 * width // batch_n // 2
+    chunks, a0, c0, r0 = [], 0, 0, 0
+    for count in (down_n, up_n + out_n, qkv_n):
+        na = max(count // 3 // 16 * 16, 16)
+        chunks.append((r0, r0 + na, r0 + count, a0, c0))
+        r0, a0, c0 = r0 + count, a0 + na, c0 + count - na
+    plan = ((0, 1, 0), (4, 2, 0), (5, 3, 0))
+    rest_plan = (
+        ((4, 0), (1, 1)),
+        (),
+        (),
+        ((5, 0), (2, 1), (3, 1), (1, 2), (4, 1), (2, 2), (5, 1), (3, 2), (4, 2), (5, 2)),
+    )
+    anywhere = pl.BlockSpec(memory_space=pl.ANY)
+    whole = pl.BlockSpec(memory_space=pltpu.VMEM)
+    low, full = jnp.bfloat16, jnp.float32
+    copies_n = 12 * len(chunks) + 31
+    output, grad_input, vector, grad_qkv, grad_out, grad_up, grad_down = pl.pallas_call(
+        functools.partial(back_kernel, chunks=tuple(chunks), plan=plan, rest_plan=rest_plan),
+        out_shape=[
+            shaped(2, block, width),
+            shaped(2, block, width),
+            shaped(16, width, kind=full),
+            shaped(width // 4, 3 * width // batch_n, kind=full),
+            shaped(width // 4, width // batch_n, kind=full),
+            shaped(width // 4, inner // batch_n, kind=full),
+            shaped(inner // 4, width // batch_n, kind=full),
+        ],
+        in_specs=[anywhere] * 13 + [whole] * 4,
+        out_specs=[whole] * 7,
+        scratch_shapes=[
+            pltpu.VMEM((width, total), full),
+            pltpu.VMEM((width, 2 * block), full),
+            pltpu.VMEM((width, total), low),
+            pltpu.VMEM((3 * half, total), low),
+            pltpu.VMEM((width, total), low),
+            pltpu.VMEM((width, total), low),
+            pltpu.VMEM((width, total), low),
+            pltpu.VMEM((2 * own_in, total), low),
+            pltpu.VMEM((3 * half, total), low),
+            pltpu.VMEM((2 * width, total), low),
+            pltpu.VMEM((2, kept_rows, block), low),
+            pltpu.VMEM((width, width), low),
+            pltpu.VMEM((own_in, width), low),
+            pltpu.VMEM((own_in, width), low),
+            pltpu.VMEM((2, z_n, 2, r0, lanes), low),
+            pltpu.VMEM((z_n, 2, a0, lanes), low),
+            pltpu.VMEM((z_n, a0, lanes), low),
+            pltpu.VMEM((2, z_n, c0, lanes), low),
+            pltpu.VMEM((z_n, c0, lanes), low),
+            pltpu.VMEM((z_n + 1, r0, lanes), low),
+            pltpu.VMEM((width, 2 * block), low),
+            pltpu.VMEM((width, 2 * block), low),
+            pltpu.VMEM((2, block, width), low),
+            pltpu.VMEM((width, 128), full),
+            pltpu.VMEM((16, width), full),
+            pltpu.VMEM((7, 16, width), full),
+            pltpu.VMEM((64, total), full),
+            pltpu.VMEM((64, total), full),
+            pltpu.VMEM((r0 - down_n, 256), low),
+            pltpu.VMEM((r0 - down_n, 256), low),
+            pltpu.VMEM((down_n // 2, lanes), low),
+            pltpu.SemaphoreType.DMA((26,)),
+            pltpu.SemaphoreType.DMA((copies_n,)),
+            pltpu.SemaphoreType.DMA((copies_n,)),
+        ],
+        compiler_params=pltpu.CompilerParams(
+            vmem_limit_bytes=62 << 20, collective_id=0, has_side_effects=True
+        ),
+        cost_estimate=pl.CostEstimate(flops=int(60e9), bytes_accessed=0, transcendentals=0),
+        name="back",
+    )(
+        ot, ot_recv, ht, at, qt, kt, vt, kept, ct, w_out, w_qkv, w_up_t, w_down_parts,
+        inv, prow, b_up_own, vecs,
+    )
+    grad_b_up = jnp.transpose(vector[10:14].reshape(2, batch_n, band), (1, 0, 2)).reshape(inner)
+    return (
+        output,
+        grad_input,
+        vector[0:5],
+        vector[5],
+        vector[6],
+        grad_qkv,
+        grad_out,
+        vector[7],
+        vector[8],
+        grad_up,
+        grad_b_up,
+        grad_down,
+        vector[9],
+    )
+
+
 def solution(mesh):
+    batch_n = mesh.shape["batch"]
+    few = mesh.shape["seq"] == 4 and batch_n == 8
+    plan = functools.partial(regrouped, batch_n=batch_n, y_n=2) if few else local
     return jax.shard_map(
-        local,
+        plan,
         mesh=mesh,
         in_specs=(
             P("batch", "seq", None),

time: 670 us -> 204 us (0.30)
  waiting for transfers between devices: 348 us -> 9.46 us
  Pallas kernels: 0 us -> 167 us
  matrix products: 144 us -> 0 us
  local copies, waits for them, and re-layouts: 74.2 us -> 19.7 us
  blocking collectives: 47.6 us -> 0 us
  other arithmetic: 36.3 us -> 2.03 us
  between operations: 15.1 us -> 0.94 us
    unnamed x16 -> x0, waiting for transfers between devices: 194 us -> none
    pallas_call x0 -> x4, Pallas kernels: none -> 167 us  [the longest x1 136 us: regrouped(): pl.pallas_call(functools.partial(back_kernel, chunks=tuple(chunks), plan=...]
    dot_general x26 -> x0, matrix products: 144 us -> none  [the longest x2 19 us: add_grads(): jnp.einsum('hqk,qhd->khd', low_chance, dout_part, preferred_element_type=...]
    reduce_scatter x6 -> x0, waiting for transfers between devices: 139 us -> none  [the longest x1 48 us: local(): lax.psum_scatter(grad_w_up.astype(jnp.bfloat16), 'seq', scatter_dimension...]
    psum x1 -> x0, blocking collectives: 41.2 us -> none  [local(): lax.psum((grad_pass, grad_ln1_gain, grad_ln1_bias, grad_ln2_gain, grad_ln...]
    slice x16 -> x3, local copies, waits for them, and re-layouts: 31.9 us -> 3.68 us  [the longest x1 1.52 us: regrouped(): vector[9]]
    another operation x8 -> x10, local copies, waits for them, and re-layouts: 18.1 us -> 2.25 us  [the longest x1 1.24 us: regrouped(): jnp.stack([2 * x + core, 2 * (1 - x) + core, 2 * x + 1 - core, 2 * (1 - x...]
    all_gather x2 -> x0, waiting for transfers between devices: 14.3 us -> none  [the longest x1 11.9 us: local(): lax.all_gather(key_flat, 'seq', axis=1, tiled=True)]
  transfers between devices with their start and end apart: 12 -> 7, of which waited for: 10 -> 1; matrix products, arithmetic and copies ran while one was open for 28% -> 2% of each run, Pallas kernels for 0% -> 15%
where the time goes in v1:
time: 204 us; the launch traced here: 203 us
  Pallas kernels  167 us (82%)
  local copies, waits for them, and re-layouts  19.7 us (10%)
  waiting for transfers between devices  9.46 us (5%)
  starting transfers between devices  4.22 us (2%)
    pallas_call x1, Pallas kernels, regrouped(): pl.pallas_call(functools.partial(back_kernel, chunks=tuple(chunks), plan=...  136 us
    pallas_call x1, Pallas kernels, regrouped(): pl.pallas_call(lambda *refs: attend_kernel(*refs[:8], *refs[8:16], refs[1...  22.9 us
    unnamed x48, local copies, waits for them, and re-layouts  10 us
    ppermute x7, waiting for transfers between devices, swap(): return lax.ppermute(array, axis, [(i, i ^ distance) for i in range(size)])  9.46 us
    pallas_call x1, Pallas kernels, regrouped(): call(prepare_kernel, [shaped(own_in, width)], n_in=2, name='prepare', flo...  5.12 us
    ppermute x7, starting transfers between devices, swap(): return lax.ppermute(array, axis, [(i, i ^ distance) for i in range(size)])  4.22 us
  transfers between devices with their start and end apart: 7, of which 1 were waited for; matrix products, arithmetic and copies ran while one was open for 2% of the time, Pallas kernels for 15%

profile of v1, /device:TPU:0, one launch (start us, length us, event | category | flops | bytes accessed | tf_op | source)
XLA Modules:
  0.0 203.2 jit_solution(5850761913301118007)
XLA Ops:
  0.7 0.8 convert_element_type.18
  1.4 1.2 fusion.1
  2.8 3.0 %collective-permute-start = (bf16[272,768]{1,0:T(8,128)(2,1)S(1)}, bf16[272,768]{1,0:T(8,128)(2,1)S(1)}, u32[]{:S(2)}, u32[]{:S(2)}) collective-permute-start(bf16[272,768]{1,0:T(8,128)(2,1)S(1)} %get-tuple-element.89), channel_id=1, source_target_pairs={{0,16},{8,24},{16,0},{24,8},{1,17},{9,25},{17,1},{25,9},{2,18},{10... | collective-permute-start | bytes 1253384 | tf_op jit(solution)/shard_map/ppermute | solution.py:1019
  5.9 0.1 collective-permute-start.4
  6.1 0.6 dynamic_slice.22
  6.8 9.4 %collective-permute-done.refs_2_ = bf16[272,768]{1,0:T(8,128)(2,1)S(1)} collective-permute-done((bf16[272,768]{1,0:T(8,128)(2,1)S(1)}, bf16[272,768]{1,0:T(8,128)(2,1)S(1)}, u32[]{:S(2)}, u32[]{:S(2)}) %collective-permute-start) | collective-permute-done | bytes 417824 | tf_op jit(solution)/shard_map/ppermute | solution.py:1019
  16.4 0.8 copy.38.refs_5_
  17.2 0.9 copy.39.refs_6_.vecs
  18.2 1.2 stack.45.refs_0_.info
  19.4 0.7 copy-done.16
  20.2 0.8 copy-done.17
  20.9 22.9 %attend.1 = (f32[768,1024]{1,0:T(8,128)}, bf16[768,1024]{1,0:T(8,128)(2,1)}, bf16[384,1024]{1,0:T(8,128)(2,1)}, bf16[384,1024]{1,0:T(8,128)(2,1)}, bf16[384,1024...) custom-call(s32[6]{0:T(128)} %stack.45.refs_0_.info, ...), custom_call_target="tpu_custom_call" | custom-call | flops 12000000000 | tf_op jit(solution)/shard_map/attend/pallas_call | solution.py:1090
  43.8 0.6 collective-permute-start.3
  44.4 0.1 collective-permute-start.5
  44.5 0.4 collective-permute-start.6
  44.9 0.1 reshape.43
  45.1 5.1 %prepare.1.w_up_in = bf16[1536,768]{1,0:T(8,128)(2,1)} custom-call(s32[6]{0:T(128)} %stack.45.refs_0_.info, bf16[768,3072]{1,0:T(8,128)(2,1)} %w_up.1), custom_call_target="tpu_custom_call" | custom-call | flops 2000000000 | tf_op jit(solution)/shard_map/prepare/pallas_call | solution.py:1076
  50.2 0.7 copy-done.18
  51.0 0.8 copy-done.19
  51.7 3.0 %turn.1.ct_in = bf16[768,1024]{1,0:T(8,128)(2,1)} custom-call(s32[6]{0:T(128)} %stack.45.refs_0_.info, bf16[256,768]{1,0:T(8,128)(2,1)} %copy-done.3, bf16[256,768]{1,0:T(8,128)(2,1)} %collective-permute-done.4.c1, bf16[256,768]{1,0:T(8,128)(2,1)} %copy-done.18, bf16[256,768]{1,0:T(8,128)(2,1)} %copy-done.19), custom_call_target="tpu_custom_call" | custom-call | flops 1000000000 | tf_op jit(solution)/shard_map/turn/pallas_call | solution.py:1128
  54.8 1.2 broadcast_in_dim.20.b_up
  55.9 135.8 %back.1 = (bf16[2,256,768]{2,1,0:T(8,128)(2,1)}, bf16[2,256,768]{2,1,0:T(8,128)(2,1)}, f32[16,768]{1,0:T(8,128)}, f32[192,288]{1,0:T(8,128)}, f32[192,96]{1,0:T(...) custom-call(bf16[384,1024]{1,0:T(8,128)(2,1)} %get-tuple-element.29.ot_own, bf16[384,1024]{1,0:T(8,128)(2,1)} %copy-done.14, ...), custom_call_target="tpu_custom_call" | custom-call | flops 60000002048 | tf_op jit(solution)/shard_map/back/pallas_call | solution.py:1149
  191.8 0.8 slice.26
  192.6 1.5 slice_reduce_fusion
  194.1 1.3 slice.21
  195.5 0.7 reshape.45
  196.2 1.9 copy.42
  198.1 2.1 %copy.50 = bf16[2,256,768]{2,1,0:T(8,128)(2,1)} copy(bf16[2,256,768]{2,1,0:T(8,128)(2,1)} %get-tuple-element.108) | data formatting | bytes 1572864
  200.2 0.9 copy.51
  201.1 0.7 copy.52
  201.8 0.6 copy.53
  202.5 0.7 copy.54
  (65 shorter events, 0.7 us)
Async XLA Ops:
  0.7 5.1 %copy-start.1 = (bf16[2,256,768]{2,1,0:T(8,128)(2,1)S(1)}, bf16[2,256,768]{2,1,0:T(8,128)(2,1)}, u32[]{:S(2)}) copy-start(bf16[2,256,768]{2,1,0:T(8,128)(2,1)} %param.29) | copy-start | bytes 2359300
  2.6 3.4 %copy-start.20 = (s32[2]{0:T(128)S(1)}, s32[2]{0:T(128)}, u32[]{:S(2)}) copy-start(s32[2]{0:T(128)} %param.16) | copy-start | bytes 28
  2.6 4.0 %copy-start.9 = (f32[768]{0:T(1024)S(1)}, f32[768]{0:T(1024)}, u32[]{:S(2)}) copy-start(f32[768]{0:T(1024)} %param.19) | copy-start | bytes 9220
  2.7 4.0 %copy-start.10 = (f32[768]{0:T(1024)S(1)}, f32[768]{0:T(1024)}, u32[]{:S(2)}) copy-start(f32[768]{0:T(1024)} %param.20) | copy-start | bytes 9220
  2.7 4.0 %copy-start.11 = (f32[768]{0:T(1024)S(1)}, f32[768]{0:T(1024)}, u32[]{:S(2)}) copy-start(f32[768]{0:T(1024)} %param.23) | copy-start | bytes 9220
  2.7 4.0 %copy-start.12 = (f32[768]{0:T(1024)S(1)}, f32[768]{0:T(1024)}, u32[]{:S(2)}) copy-start(f32[768]{0:T(1024)} %param.24) | copy-start | bytes 9220
  2.7 4.0 %copy-start.13 = (f32[768]{0:T(1024)S(1)}, f32[768]{0:T(1024)}, u32[]{:S(2)}) copy-start(f32[768]{0:T(1024)} %param.28) | copy-start | bytes 9220
  2.7 4.1 %copy-start.7 = (f32[5,768]{1,0:T(8,128)S(1)}, f32[5,768]{1,0:T(8,128)}, u32[]{:S(2)}) copy-start(f32[5,768]{1,0:T(8,128)} %param.18) | copy-start | bytes 46084
  2.8 16.6 %copy-start.2 = (bf16[272,768]{1,0:T(8,128)(2,1)}, bf16[272,768]{1,0:T(8,128)(2,1)S(1)}, u32[]{:S(2)}) copy-start(bf16[272,768]{1,0:T(8,128)(2,1)S(1)} %get-tuple-element.90.refs_1_) | copy-start | bytes 1253380
  2.8 13.5 %collective-permute-start = (bf16[272,768]{1,0:T(8,128)(2,1)S(1)}, bf16[272,768]{1,0:T(8,128)(2,1)S(1)}, u32[]{:S(2)}, u32[]{:S(2)}) collective-permute-start(bf16[272,768]{1,0:T(8,128)(2,1)S(1)} %get-tuple-element.89), channel_id=1, source_target_pairs={{0,16},{8,24},{16,0},{24,8},{1,17},{9,25},{17,1},{25,9},{2,18},{10... | collective-permute-start | bytes 1253384 | tf_op jit(solution)/shard_map/ppermute | solution.py:1019
  5.9 38.5 %copy-start.3 = (bf16[256,768]{1,0:T(8,128)(2,1)}, bf16[256,768]{1,0:T(8,128)(2,1)S(1)}, u32[]{:S(2)}) copy-start(bf16[256,768]{1,0:T(8,128)(2,1)S(1)} %get-tuple-element.92.c0) | copy-start | bytes 1179652
  5.9 38.6 %collective-permute-start.4 = (bf16[256,768]{1,0:T(8,128)(2,1)S(1)}, bf16[256,768]{1,0:T(8,128)(2,1)}, u32[]{:S(2)}, u32[]{:S(2)}) collective-permute-start(bf16[256,768]{1,0:T(8,128)(2,1)S(1)} %get-tuple-element.91), channel_id=1, source_target_pairs={{0,16},{8,24},{16,0},{24,8},{1,17},{9,25},{17,1},{25,9},{2,18},{10... | collective-permute-start | bytes 1179656 | tf_op jit(solution)/shard_map/ppermute | solution.py:1019
  6.0 13.4 %collective-permute-start.1 = (bf16[272,768]{1,0:T(8,128)(2,1)S(1)}, bf16[272,768]{1,0:T(8,128)(2,1)S(1)}, u32[]{:S(2)}, u32[]{:S(2)}) collective-permute-start(bf16[272,768]{1,0:T(8,128)(2,1)S(1)} %get-tuple-element.90.refs_1_), channel_id=1, source_target_pairs={{0,8},{8,0},{16,24},{24,16},{1,9},{9,1},{17,25},{25,17},{2,10},{10... | collective-permute-start | bytes 1253384 | tf_op jit(solution)/shard_map/ppermute | solution.py:1019
  16.3 3.2 %copy-start.15 = (bf16[272,768]{1,0:T(8,128)(2,1)}, bf16[272,768]{1,0:T(8,128)(2,1)S(1)}, u32[]{:S(2)}) copy-start(bf16[272,768]{1,0:T(8,128)(2,1)S(1)} %collective-permute-done.refs_2_) | copy-start | bytes 1253380
  16.3 3.1 %collective-permute-start.2 = (bf16[272,768]{1,0:T(8,128)(2,1)S(1)}, bf16[272,768]{1,0:T(8,128)(2,1)S(1)}, u32[]{:S(2)}, u32[]{:S(2)}) collective-permute-start(bf16[272,768]{1,0:T(8,128)(2,1)S(1)} %collective-permute-done.refs_2_), channel_id=1, source_target_pairs={{0,8},{8,0},{16,24},{24,16},{1,9},{9,1},{17,25},{25,17},{2,10},{10... | collective-permute-start | bytes 1253384 | tf_op jit(solution)/shard_map/ppermute | solution.py:1019
  19.4 25.5 %copy-start.8 = (f32[3072]{0:T(1024)S(1)}, f32[3072]{0:T(1024)}, u32[]{:S(2)}) copy-start(f32[3072]{0:T(1024)} %param.26) | copy-start | bytes 36868
  19.4 0.8 copy-start.16
  20.2 0.8 copy-start.17
  43.8 10.9 %collective-permute-start.3 = (bf16[384,1024]{1,0:T(8,128)(2,1)}, bf16[384,1024]{1,0:T(8,128)(2,1)S(1)}, u32[]{:S(2)}, u32[]{:S(2)}) collective-permute-start(bf16[384,1024]{1,0:T(8,128)(2,1)} %get-tuple-element.29.ot_own), channel_id=1, source_target_pairs={{0,8},{8,0},{16,24},{24,16},{1,9},{9,1},{17,25},{25,17},{2,10},{10... | collective-permute-start | bytes 2359304 | tf_op jit(solution)/shard_map/ppermute | solution.py:1019
  44.4 5.8 %collective-permute-start.5 = (bf16[256,768]{1,0:T(8,128)(2,1)S(1)}, bf16[256,768]{1,0:T(8,128)(2,1)S(1)}, u32[]{:S(2)}, u32[]{:S(2)}) collective-permute-start(bf16[256,768]{1,0:T(8,128)(2,1)S(1)} %get-tuple-element.92.c0), channel_id=1, source_target_pairs={{0,8},{8,0},{16,24},{24,16},{1,9},{9,1},{17,25},{25,17},{2,10},{10... | collective-permute-start | bytes 1179656 | tf_op jit(solution)/shard_map/ppermute | solution.py:1019
  44.5 5.7 %collective-permute-start.6 = (bf16[256,768]{1,0:T(8,128)(2,1)}, bf16[256,768]{1,0:T(8,128)(2,1)S(1)}, u32[]{:S(2)}, u32[]{:S(2)}) collective-permute-start(bf16[256,768]{1,0:T(8,128)(2,1)} %collective-permute-done.4.c1), channel_id=1, source_target_pairs={{0,8},{8,0},{16,24},{24,16},{1,9},{9,1},{17,25},{25,17},{2,10},{10... | collective-permute-start | bytes 1179656 | tf_op jit(solution)/shard_map/ppermute | solution.py:1019
  50.2 0.8 copy-start.18
  51.0 0.8 copy-start.19
  54.8 1.2 copy-start.14
  191.8 8.5 %copy-start = (bf16[2,256,768]{2,1,0:T(8,128)(2,1)S(1)}, bf16[2,256,768]{2,1,0:T(8,128)(2,1)}, u32[]{:S(2)}) copy-start(bf16[2,256,768]{2,1,0:T(8,128)(2,1)} %get-tuple-element.109) | copy-start | bytes 2359300
  198.1 3.0 %copy-start.5 = (f32[192,288]{1,0:T(8,128)S(1)}, f32[192,288]{1,0:T(8,128)}, u32[]{:S(2)}) copy-start(f32[192,288]{1,0:T(8,128)} %get-tuple-element.113) | copy-start | bytes 663556
  198.1 3.7 %copy-start.6 = (f32[192,96]{1,0:T(8,128)S(1)}, f32[192,96]{1,0:T(8,128)}, u32[]{:S(2)}) copy-start(f32[192,96]{1,0:T(8,128)} %get-tuple-element.114) | copy-start | bytes 221188
  198.1 4.4 %copy-start.4 = (f32[192,384]{1,0:T(8,128)S(1)}, f32[192,384]{1,0:T(8,128)}, u32[]{:S(2)}) copy-start(f32[192,384]{1,0:T(8,128)} %get-tuple-element.117) | copy-start | bytes 884740
